TPU v7x, 32 devices: a whole 2x2x4 slice. The times are simulated.
32 devices in a mesh: groups: 1, expert: 16 (over z, y, core), dp: 2 (over x).
Axes of the slice: x: 2, y: 2, z: 4, core: 2. Of those that a mesh axis runs over, the one named last changes fastest.
Arguments:
- tokens: bfloat16 [768, 2048], P(('groups', 'expert', 'dp')), may hold values from -6 to 6
- targets: bfloat16 [768, 2048], P(('groups', 'expert', 'dp')), may hold values from -6 to 6
- expert_ids: int32 [768, 8], P(('groups', 'expert', 'dp')), may hold values from 0 to 15, all different within a row; in each aligned block of 24 rows (0 to 23, 24 to 47, ...) at most 13 rows name the same one
- gate_codes: int32 [768, 8], P(('groups', 'expert', 'dp')), may hold values from 1 to 255
- projections: bfloat16 [16, 2, 2048, 768], P('expert', None, None, 'dp'), may hold values from -0.125 to 0.125
- down_weight: bfloat16 [16, 768, 2048], P('expert', 'dp'), may hold values from -0.21875 to 0.21875
- direction: bfloat16 [16, 2048, 768], P('expert', None, 'dp'), may hold values from -0.125 to 0.125
Outputs:
- hvp: bfloat16 [16, 2048, 768], P(('groups', 'expert'), None, 'dp')
Inputs may be any that keep to these rules, and one draw needn't show every extreme that they name: `expert_ids`: each row names 8 different experts. In each aligned block of 24 rows (the tokens of one device) no expert is named by more than 13 rows, and in some block one expert is named by exactly 13.
All inputs are finite; a program needn't handle non-finite values.
Results may differ from a plain program's by a relative error of at most 0.01.
Values may be sent and summed in bfloat16 or wider, within the bound.
A program may use at most 64 MiB of HBM per device.

v0:
```python
import math

import jax
import jax.numpy as jnp
from jax import lax
from jax.sharding import PartitionSpec as P


def slot_tables(route_ids, expert_total, slot_cap):
    routed_flat = route_ids.reshape(-1)
    route_count = routed_flat.shape[0]
    onehot = (routed_flat[:, None] == jnp.arange(expert_total, dtype=jnp.int32)[None, :]).astype(
        jnp.int32
    )
    earlier = jnp.cumsum(onehot, axis=0) - onehot
    within_slot = jnp.sum(earlier * onehot, axis=1)
    landing = routed_flat * slot_cap + within_slot
    source_route = (
        jnp.zeros((expert_total * slot_cap,), jnp.int32)
        .at[landing]
        .set(jnp.arange(route_count, dtype=jnp.int32))
    )
    occupied = jnp.zeros((expert_total * slot_cap,), jnp.int32).at[landing].set(1)
    return (landing, source_route, occupied)


def body(tokens, targets, expert_ids, gate_codes, projections, down_weight, direction):
    tok_rows, model_width = tokens.shape
    top_count = expert_ids.shape[1]
    local_experts = projections.shape[0]
    expert_devs = lax.axis_size("expert")
    all_experts = local_experts * expert_devs
    slot_cap = max(2, tok_rows * top_count // all_experts + 1)
    landing, source_route, occupied = slot_tables(expert_ids, all_experts, slot_cap)
    source_token = source_route // top_count
    send_rows = jnp.where(occupied[:, None] > 0, tokens[source_token], jnp.zeros((), tokens.dtype))
    send_rows = send_rows.reshape(expert_devs, local_experts, slot_cap, model_width)
    arrived = lax.all_to_all(send_rows, "expert", split_axis=0, concat_axis=0, tiled=True)
    pair_pre = jnp.einsum(
        "sxcd,xkdf->ksxcf",
        arrived,
        lax.all_gather(projections, "dp", axis=3, tiled=True),
        preferred_element_type=jnp.float32,
    )
    tangent_pre = jnp.einsum(
        "sxcd,xdf->sxcf",
        arrived,
        lax.all_gather(direction, "dp", axis=2, tiled=True),
        preferred_element_type=jnp.float32,
    )
    gate_pre = pair_pre[0]
    up_pre = pair_pre[1]
    down_full = lax.all_gather(down_weight, "dp", axis=1, tiled=True)
    sigmoid_val = jax.nn.sigmoid(gate_pre)
    first_slope = sigmoid_val * (1.0 + gate_pre * (1.0 - sigmoid_val))
    second_slope = sigmoid_val * (1.0 - sigmoid_val) * (2.0 + gate_pre * (1.0 - 2.0 * sigmoid_val))
    hidden = (gate_pre * sigmoid_val * up_pre).astype(jnp.bfloat16)
    hidden_tan = (first_slope * tangent_pre * up_pre).astype(jnp.bfloat16)
    stacked_hidden = jnp.stack([hidden, hidden_tan])
    expert_out = jnp.einsum(
        "ksxcf,xfd->ksxcd", stacked_hidden, down_full, preferred_element_type=jnp.float32
    ).astype(jnp.bfloat16)
    returned = lax.all_to_all(expert_out, "expert", split_axis=1, concat_axis=1, tiled=True)
    slot_out = returned.reshape(2, all_experts * slot_cap, model_width)
    route_out = slot_out[:, landing].astype(jnp.float32)
    route_weight = gate_codes.reshape(-1).astype(jnp.float32) / 256.0
    combined = jnp.sum(
        (route_out * route_weight[None, :, None]).reshape(2, tok_rows, top_count, model_width),
        axis=2,
    )
    residual = combined[0] - targets.astype(jnp.float32)
    pair_res = jnp.stack([residual, combined[1]])
    slot_weight = jnp.where(occupied > 0, route_weight[source_route], jnp.zeros((), jnp.float32))
    outgoing = (pair_res[:, source_token] * slot_weight[None, :, None]).astype(jnp.bfloat16)
    outgoing = outgoing.reshape(2, expert_devs, local_experts, slot_cap, model_width)
    incoming = lax.all_to_all(outgoing, "expert", split_axis=1, concat_axis=1, tiled=True)
    grad_hidden = jnp.einsum(
        "ksxcd,xfd->ksxcf", incoming, down_full, preferred_element_type=jnp.float32
    )
    hess_pre = (
        grad_hidden[1] * up_pre * first_slope + grad_hidden[0] * up_pre * second_slope * tangent_pre
    ).astype(jnp.bfloat16)
    partial_sum = jnp.einsum(
        "sxcd,sxcf->xdf", arrived, hess_pre, preferred_element_type=jnp.float32
    )
    summed = lax.psum_scatter(
        partial_sum.astype(jnp.bfloat16), "dp", scatter_dimension=2, tiled=True
    ).astype(jnp.float32)
    loss_scale = 1.0 / math.sqrt(tok_rows * top_count)
    return (summed * loss_scale).astype(jnp.bfloat16)


def solution(mesh):
    return jax.shard_map(
        body,
        mesh=mesh,
        in_specs=(
            P(("groups", "expert", "dp"), None),
            P(("groups", "expert", "dp"), None),
            P(("groups", "expert", "dp"), None),
            P(("groups", "expert", "dp"), None),
            P("expert", None, None, "dp"),
            P("expert", "dp", None),
            P("expert", None, "dp"),
        ),
        out_specs=P(("groups", "expert"), None, "dp"),
        check_vma=False,
    )
```

profile of v0, /device:TPU:0, one launch (start us, length us, event | category | flops | bytes accessed | tf_op | source)
XLA Modules:
  0.0 392.6 jit_solution(14286486730259228713)
XLA Ops:
  6.5 0.7 all-gather.6.cloned.1.call-update
  7.3 0.7 all-gather.4.cloned.1.call-update
  8.1 0.7 all-gather.8.cloned.1.call-update
  8.8 0.1 eq.22
  8.9 0.6 reduce-window.6
  9.5 0.2 slice_reduce_fusion
  9.8 0.1 bitcast_bitcast_fusion
  9.9 0.1 mul.192
  10.1 1.2 scatter_custom_fusion.1
  11.4 0.1 div.51
  11.5 1.2 scatter_custom_fusion
  12.7 1.9 gather_fusion.3
  14.7 0.1 broadcast_in_dim.36
  14.8 1.2 gather_fusion
  16.0 0.3 gather.17
  16.3 0.1 select_bitcast_fusion
  16.4 32.0 %all_to_all.15 = bf16[16,1,13,2048]{3,2,1,0:T(8,128)(2,1)S(1)} all-to-all(bf16[16,1,13,2048]{3,2,1,0:T(8,128)(2,1)S(1)} %select_bitcast_fusion), channel_id=1, replica_groups=mesh['groups'=1,'expert'=16,'dp'=2] {'expert'}, dimensions={0} | all-to-all | bytes 1703936 | tf_op jit(solution)/shard_map/all_to_all | solution.py:38
  48.4 8.2 %all-gather.6.cloned.1.call-done = bf16[1,2048,768]{2,1,0:T(8,128)(2,1)} async-done(((bf16[1,2048,384]{2,1,0:T(8,128)(2,1)}), bf16[1,2048,768]{2,1,0:T(8,128)(2,1)}) %all-gather.6.cloned.1.call-update) | async-done | bytes 3145744 | tf_op jit(solution)/shard_map/all_gather | solution.py:48
  56.6 3.2 fusion.26
  59.8 78.8 %all-gather.4.cloned.1.call-done = bf16[1,2,2048,768]{3,2,1,0:T(8,128)(2,1)} async-done(((bf16[1,2,2048,384]{3,2,1,0:T(8,128)(2,1)}), bf16[1,2,2048,768]{3,2,1,0:T(8,128)(2,1)}) %all-gather.4.cloned.1.call-update) | async-done | bytes 6291472 | tf_op jit(solution)/shard_map/all_gather | solution.py:42
  138.6 4.5 %fusion.23 = f32[2,16,1,13,768]{4,1,0,3,2:T(8,128)S(1)} fusion(bf16[1,2,2048,768]{3,2,1,0:T(8,128)(2,1)} %all-gather.4.cloned.1.call-done, bf16[16,1,13,2048]{3,2,1,0:T(8,128)(2,1)S(1)} %all_to_all.15), kind=kOutput, calls=%fused_computation.27 | convolution fusion | flops 1308622848 | bytes 8421376 | tf_op jit(solution)/shard_map/sxcd,xkdf->ksxcf/dot_general | solution.py:39
  143.1 0.2 fusion.53
  143.3 0.8 copy-done.1
  144.1 0.3 fusion.57
  144.4 40.7 %all-gather.8.cloned.1.call-done = bf16[1,768,2048]{2,1,0:T(8,128)(2,1)} async-done(((bf16[1,384,2048]{2,1,0:T(8,128)(2,1)}), bf16[1,768,2048]{2,1,0:T(8,128)(2,1)}) %all-gather.8.cloned.1.call-update) | async-done | bytes 3145744 | tf_op jit(solution)/shard_map/all_gather | solution.py:53
  185.1 3.4 fusion.12
  188.5 3.0 copy.48
  191.4 5.6 %all-to-all-start.1 = ((bf16[2,16,1,13,2048]{4,0,3,2,1:T(2,128)(2,1)}), bf16[2,16,1,13,2048]{4,0,3,2,1:T(2,128)(2,1)S(1)}, u32[]{:S(2)}, u32[]{:S(2)}) async-start(bf16[2,16,1,13,2048]{4,0,3,2,1:T(2,128)(2,1)} %copy.48), calls=%async_computation.1 | async-start | bytes 3407872 | tf_op jit(solution)/shard_map/all_to_all | solution.py:63
  197.1 0.2 reduce-scatter.4.cloned.1.call-start
  197.3 0.1 mul.202
  197.4 33.9 %all-to-all-done.1 = bf16[2,16,1,13,2048]{4,0,3,2,1:T(2,128)(2,1)S(1)} async-done(((bf16[2,16,1,13,2048]{4,0,3,2,1:T(2,128)(2,1)}), bf16[2,16,1,13,2048]{4,0,3,2,1:T(2,128)(2,1)S(1)}, u32[]{:S(2)}, u32[]{:S(2)}) %all-to-all-start.1) | async-done | bytes 1703968 | tf_op jit(solution)/shard_map/all_to_all | solution.py:63
  231.3 10.5 %gather_fusion.1 = bf16[192,2,2048]{2,1,0:T(2,128)(2,1)S(1)} fusion(bf16[2,208,2048]{2,0,1:T(2,128)(2,1)S(1)} %bitcast.197, s32[1024]{0:T(1024)S(1)} %pad_clamp_fusion.1), kind=kCustom, calls=%fused_computation.1 | custom fusion | bytes 3146496 | tf_op jit(solution)/shard_map/gather | solution.py:65
  241.9 1.8 convert_element_type.86
  243.7 2.2 multiply_reduce_fusion
  245.9 0.3 fusion.72
  246.3 0.2 copy.50
  246.5 0.4 pad_maximum_fusion
  246.9 10.9 %gather_fusion.2 = f32[208,2,2048]{2,1,0:T(2,128)} fusion(f32[2,24,2048]{2,0,1:T(2,128)S(1)} %pad_maximum_fusion, s32[1024]{0:T(1024)S(1)} %get-tuple-element.12), kind=kCustom, calls=%fused_computation.2 | custom fusion | bytes 6816576 | tf_op jit(solution)/shard_map/gather | solution.py:74
  257.8 3.4 fusion.15
  261.2 50.2 %all_to_all.16 = bf16[2,16,1,13,2048]{4,0,3,2,1:T(2,128)(2,1)S(1)} all-to-all(bf16[2,16,1,13,2048]{4,0,3,2,1:T(2,128)(2,1)S(1)} %fusion.15), channel_id=1, replica_groups=mesh['groups'=1,'expert'=16,'dp'=2] {'expert'}, dimensions={1} | all-to-all | bytes 3407872 | tf_op jit(solution)/shard_map/all_to_all | solution.py:76
  311.4 2.3 fusion.18
  313.7 1.8 fusion.8
  315.4 11.5 %copy.56 = bf16[1,2048,768]{1,0,2:T(2,128)(2,1)} copy(bf16[1,2048,768]{2,1,0:T(8,128)(2,1)S(1)} %fusion.8) | data formatting | bytes 6291456
  326.9 6.4 %copy.85 = bf16[768,1,2048]{2,0,1:T(8,128)(2,1)} copy(bf16[768,1,2048]{2,1,0:T(2,128)(2,1)} %bitcast.193) | data formatting | bytes 6291456
  333.4 41.2 %reduce-scatter.4.cloned.1.call-done = bf16[384,2048]{1,0:T(8,128)(2,1)} async-done(((bf16[768,2048]{1,0:T(8,128)(2,1)}), bf16[384,2048]{1,0:T(8,128)(2,1)}) %reduce-scatter.4.cloned.1.call-update) | async-done | bytes 1572880
  374.6 3.3 reshape_bitcast_fusion
  377.9 5.2 %copy.57 = bf16[1,2048,384]{2,1,0:T(8,128)(2,1)} copy(bf16[1,2048,384]{1,0,2:T(2,128)(2,1)S(1)} %reshape_bitcast_fusion) | data formatting | bytes 3145728
  383.2 2.9 multiply_convert_fusion.1
  (43 shorter events, 0.6 us)
Async XLA Ops:
  6.5 8.2 %copy-start = (bf16[24,2048]{1,0:T(8,128)(2,1)S(1)}, bf16[24,2048]{1,0:T(8,128)(2,1)}, u32[]{:S(2)}) copy-start(bf16[24,2048]{1,0:T(8,128)(2,1)} %param.7) | copy-start | bytes 294916
  6.5 2.2 copy-start.8
  6.5 4.7 %copy-start.9 = (s32[24,8]{0,1:T(8,128)S(1)}, s32[24,8]{0,1:T(8,128)}, u32[]{:S(2)}) copy-start(s32[24,8]{0,1:T(8,128)} %param.10) | copy-start | bytes 2308
  6.5 50.1 %all-gather.6.cloned.1.call-start = ((), (), s32[]{:S(2)}) async-start(), calls=%async_computation.5 | async-start | bytes 4718592 | tf_op jit(solution)/shard_map/all_gather | solution.py:48
  7.3 131.3 %all-gather.4.cloned.1.call-start = ((), (), s32[]{:S(2)}) async-start(), calls=%async_computation.4 | async-start | bytes 9437184 | tf_op jit(solution)/shard_map/all_gather | solution.py:42
  8.0 177.1 %all-gather.8.cloned.1.call-start = ((), (), s32[]{:S(2)}) async-start(), calls=%async_computation.6 | async-start | bytes 4718592 | tf_op jit(solution)/shard_map/all_gather | solution.py:53
  48.4 90.1 %copy-start.3 = (bf16[16,1,13,2048]{3,2,1,0:T(8,128)(2,1)}, bf16[16,1,13,2048]{3,2,1,0:T(8,128)(2,1)S(1)}, u32[]{:S(2)}) copy-start(bf16[16,1,13,2048]{3,2,1,0:T(8,128)(2,1)S(1)} %all_to_all.15) | copy-start | bytes 2555908
  59.8 83.5 %copy-start.5 = (f32[16,1,13,768]{3,0,2,1:T(8,128)}, f32[16,1,13,768]{3,0,2,1:T(8,128)S(1)}, u32[]{:S(2)}) copy-start(f32[16,1,13,768]{3,0,2,1:T(8,128)S(1)} %fusion.26) | copy-start | bytes 1916932
  143.1 1.0 copy-start.1
  191.4 39.9 %all-to-all-start.1 = ((bf16[2,16,1,13,2048]{4,0,3,2,1:T(2,128)(2,1)}), bf16[2,16,1,13,2048]{4,0,3,2,1:T(2,128)(2,1)S(1)}, u32[]{:S(2)}, u32[]{:S(2)}) async-start(bf16[2,16,1,13,2048]{4,0,3,2,1:T(2,128)(2,1)} %copy.48), calls=%async_computation.1 | async-start | bytes 3407872 | tf_op jit(solution)/shard_map/all_to_all | solution.py:63
  197.1 177.5 %reduce-scatter.4.cloned.1.call-start = ((), (), s32[]{:S(2)}) async-start(), calls=%async_computation.7 | async-start | bytes 4718592
  243.7 2.5 copy-start.7
  257.8 53.5 %copy-start.10 = (bf16[1,768,2048]{2,1,0:T(8,128)(2,1)S(1)}, bf16[1,768,2048]{2,1,0:T(8,128)(2,1)}, u32[]{:S(2)}) copy-start(bf16[1,768,2048]{2,1,0:T(8,128)(2,1)} %all-gather.8.cloned.1.call-done) | copy-start | bytes 9437188
  311.3 2.3 copy-start.2
  311.3 2.3 copy-start.4
  311.3 2.3 copy-start.6
Sparse Core Ops, SparseCore 0:
  8.9 47.6 all-gather.5
  58.2 80.3 all-gather.3
  140.1 44.9 all-gather.7
  333.5 41.0 reduce-scatter.3
where the time goes:
time: 393 us
  waiting for transfers between devices  205 us (52%)
  blocking collectives  82.2 us (21%)
  local copies, waits for them, and re-layouts  58.9 us (15%)
  matrix products  15.1 us (4%)
  between operations  13.5 us (3%)
  other arithmetic  12.1 us (3%)
  starting transfers between devices  5.92 us (2%)
    all_gather x1, waiting for transfers between devices, body(): lax.all_gather(projections, 'dp', axis=3, tiled=True)  78.8 us
    all_to_all x1, blocking collectives, body(): lax.all_to_all(outgoing, 'expert', split_axis=1, concat_axis=1, tiled=True)  50.2 us
    unnamed x5, waiting for transfers between devices  43.3 us
    all_gather x1, waiting for transfers between devices, body(): down_full = lax.all_gather(down_weight, 'dp', axis=1, tiled=True)  40.7 us
    all_to_all x1, waiting for transfers between devices, body(): lax.all_to_all(expert_out, 'expert', split_axis=1, concat_axis=1, tiled=T...  33.9 us
    all_to_all x1, blocking collectives, body(): lax.all_to_all(send_rows, 'expert', split_axis=0, concat_axis=0, tiled=True)  32 us
    unnamed x27, local copies, waits for them, and re-layouts  27.4 us
    gather x1, local copies, waits for them, and re-layouts, body(): pair_res[:, source_token] * slot_weight[None, :, None]  10.9 us
  transfers between devices with their start and end apart: 5, of which 5 were waited for; matrix products, arithmetic and copies ran while one was open for 4% of the time, Pallas kernels for 0%

commit v1 on v0

--- a/solution.py
+++ b/solution.py
@@ -1,9 +1,321 @@
+import functools
 import math
 
 import jax
 import jax.numpy as jnp
 from jax import lax
+from jax.experimental import pallas as pl
+from jax.experimental.pallas import tpu as pltpu
 from jax.sharding import PartitionSpec as P
+
+LINE = 4
+VMEM_BYTES = 56 * 1024 * 1024
+DENSE_BYTES = 16 * 1024 * 1024
+
+
+class Place:
+    def __init__(self):
+        expert = lax.axis_index("expert")
+        self.z = expert // 4
+        self.y = lax.rem(expert // 2, 2)
+        self.c = lax.rem(expert, 2)
+        self.x = lax.axis_index("dp")
+
+    def line(self, d):
+        return lax.rem(self.z + d, LINE)
+
+    def device(self, z, y, c, x):
+        return {"expert": (z * 2 + y) * 2 + c, "dp": x}
+
+    def along_z(self, d):
+        return self.device(self.line(d), self.y, self.c, self.x)
+
+    def along_y(self):
+        return self.device(self.z, 1 - self.y, self.c, self.x)
+
+    def along_x(self):
+        return self.device(self.z, self.y, self.c, 1 - self.x)
+
+    def sibling(self):
+        return self.device(self.z, self.y, 1 - self.c, self.x)
+
+    def greet(self):
+        barrier = pltpu.get_barrier_semaphore()
+        others = [self.along_z(d) for d in range(1, LINE)]
+        others += [self.along_y(), self.along_x(), self.sibling()]
+        for other in others:
+            pl.semaphore_signal(
+                barrier, inc=1, device_id=other, device_id_type=pl.DeviceIdType.MESH
+            )
+        pl.semaphore_wait(barrier, len(others))
+
+
+def remote(src, dst, send_sem, recv_sem, to):
+    return pltpu.make_async_remote_copy(
+        src_ref=src,
+        dst_ref=dst,
+        send_sem=send_sem,
+        recv_sem=recv_sem,
+        device_id=to,
+        device_id_type=pl.DeviceIdType.MESH,
+    )
+
+
+def spread(me, pieces, send_sem, recv_sem):
+    sends = []
+
+    def copy(p, block, to, number):
+        ref = pieces[p][0](*block)
+        return remote(ref, ref, send_sem.at[number], recv_sem.at[(p,) + block], to)
+
+    def push(p, block, to):
+        item = copy(p, block, to, len(sends))
+        item.start()
+        sends.append(item)
+
+    def arrive(p, block):
+        copy(p, block, me.sibling(), 0).wait_recv()
+
+    count = range(len(pieces))
+    ways = [
+        (me.along_y(), me.along_x()) if first == "y" else (me.along_x(), me.along_y())
+        for _, first in pieces
+    ]
+    own = (me.z, me.y, me.c, me.x)
+    for d in (2, 1, 3):
+        for p in count:
+            push(p, own, me.along_z(d))
+    for d in range(LINE):
+        z = me.line(d)
+        for p in count:
+            block = (z, me.y, me.c, me.x)
+            if d:
+                arrive(p, block)
+            push(p, block, ways[p][0])
+            push(p, block, ways[p][1])
+            push(p, block, me.sibling())
+        for p in count:
+            y_first = pieces[p][1] == "y"
+            block = (z, 1 - me.y, me.c, me.x) if y_first else (z, me.y, me.c, 1 - me.x)
+            arrive(p, block)
+            push(p, block, ways[p][1])
+            push(p, block, me.sibling())
+    for d in range(LINE):
+        z = me.line(d)
+        for p in count:
+            y_first = pieces[p][1] == "y"
+            near = (z, me.y, me.c, 1 - me.x) if y_first else (z, 1 - me.y, me.c, me.x)
+            for block in (near, (z, 1 - me.y, me.c, 1 - me.x)):
+                arrive(p, block)
+                push(p, block, me.sibling())
+    for d in range(LINE):
+        for p in count:
+            for y in range(2):
+                for x in range(2):
+                    arrive(p, (me.line(d), y, 1 - me.c, x))
+    for item in sends:
+        item.wait_send()
+
+
+SPREAD_SENDS = 3 + LINE * 5 + LINE * 2
+
+
+def gather_kernel(tok_ref, weight_ref, all_tok, all_weight, send_sem, recv_sem):
+    me = Place()
+    half = tok_ref.shape[1] // 2
+    all_tok[me.z, me.y, me.c, me.x] = tok_ref[...]
+    all_weight[me.z, me.y, me.c, me.x] = weight_ref[...]
+    me.greet()
+    pieces = [
+        (lambda z, y, c, x: all_tok.at[z, y, c, x, :, pl.ds(0, half)], "y"),
+        (lambda z, y, c, x: all_tok.at[z, y, c, x, :, pl.ds(half, half)], "x"),
+        (lambda z, y, c, x: all_weight.at[z, y, c, x], "y"),
+    ]
+    spread(me, pieces, send_sem, recv_sem)
+
+
+def gather_tokens(tokens, weights):
+    rows, width = tokens.shape
+    grid = (LINE, 2, 2, 2)
+    vmem = pl.BlockSpec(memory_space=pltpu.VMEM)
+    return pl.pallas_call(
+        gather_kernel,
+        out_shape=(
+            jax.ShapeDtypeStruct(grid + (rows, width), tokens.dtype),
+            jax.ShapeDtypeStruct(grid + weights.shape, weights.dtype),
+        ),
+        in_specs=[vmem] * 2,
+        out_specs=(vmem, vmem),
+        scratch_shapes=[
+            pltpu.SemaphoreType.DMA((3 * SPREAD_SENDS,)),
+            pltpu.SemaphoreType.DMA((3,) + grid),
+        ],
+        compiler_params=pltpu.CompilerParams(
+            collective_id=0, has_side_effects=True, vmem_limit_bytes=VMEM_BYTES
+        ),
+    )(tokens, weights)
+
+
+def exchange_kernel(
+    part, targets, out, core_in, out1, in1, out2, in2, out3, in3,
+    core_send, core_recv, send1, recv1, send2, recv2, send3, recv3, send_sem, recv_sem,
+):
+    me = Place()
+    half = targets.shape[1] // 2
+    me.greet()
+    sends = []
+
+    def push(src, dst, send, recv, to):
+        item = remote(src, dst, send, recv, to)
+        item.start()
+        sends.append(item)
+        return item
+
+    turn = (1, 2, 3, 0)
+    core_copies = {}
+    for d in turn:
+        z = me.line(d)
+        core_copies[d] = push(
+            part.at[:, z, :, 1 - me.c], core_in.at[:, z], core_send.at[d], core_recv.at[d],
+            me.sibling(),
+        )
+
+    def pair(h, z, far, near):
+        cols = pl.ds(h * half, half)
+        y, x = (near, far) if h == 0 else (far, near)
+        mine = part[:, z, y, me.c, x, :, cols].astype(jnp.float32)
+        return mine + core_in[:, z, y, x, :, cols].astype(jnp.float32)
+
+    axis1 = (me.along_x(), me.along_y())
+    axis2 = (me.along_y(), me.along_x())
+    far_own = (me.x, me.y)
+    near_own = (me.y, me.x)
+    first, second, third = {}, {}, {}
+    for d in turn:
+        z = me.line(d)
+        core_copies[d].wait_recv()
+        for h in range(2):
+            for near in range(2):
+                out1[h, d, near] = pair(h, z, 1 - far_own[h], near).astype(out1.dtype)
+            first[d, h] = push(
+                out1.at[h, d], in1.at[h, d], send1.at[h, d], recv1.at[h, d], axis1[h]
+            )
+    for d in turn:
+        z = me.line(d)
+        for h in range(2):
+            first[d, h].wait_recv()
+            near = 1 - near_own[h]
+            total = pair(h, z, far_own[h], near) + in1[h, d, near].astype(jnp.float32)
+            out2[h, d] = total.astype(out2.dtype)
+            second[d, h] = push(
+                out2.at[h, d], in2.at[h, d], send2.at[h, d], recv2.at[h, d], axis2[h]
+            )
+    held = [None, None]
+    for d in turn:
+        z = me.line(d)
+        for h in range(2):
+            second[d, h].wait_recv()
+            near = near_own[h]
+            total = pair(h, z, far_own[h], near) + in1[h, d, near].astype(jnp.float32)
+            total = total + in2[h, d].astype(jnp.float32)
+            if d:
+                out3[h, d - 1] = total.astype(out3.dtype)
+                third[d, h] = push(
+                    out3.at[h, d - 1], in3.at[h, d - 1], send3.at[h, d - 1], recv3.at[h, d - 1],
+                    me.along_z(d),
+                )
+            else:
+                held[h] = total
+    for h in range(2):
+        cols = pl.ds(h * half, half)
+        total = held[h]
+        for d in range(1, LINE):
+            third[d, h].wait_recv()
+            total = total + in3[h, d - 1].astype(jnp.float32)
+        residual = total[0] - targets[:, cols].astype(jnp.float32)
+        out[0, me.z, me.y, me.c, me.x, :, cols] = residual.astype(out.dtype)
+        out[1, me.z, me.y, me.c, me.x, :, cols] = total[1].astype(out.dtype)
+    pieces = [
+        (lambda z, y, c, x: out.at[:, z, y, c, x, :, pl.ds(0, half)], "y"),
+        (lambda z, y, c, x: out.at[:, z, y, c, x, :, pl.ds(half, half)], "x"),
+    ]
+    spread(me, pieces, send_sem, recv_sem)
+    for item in sends:
+        item.wait_send()
+
+
+def exchange(part, targets):
+    rows, width = targets.shape
+    half = width // 2
+    grid = (LINE, 2, 2, 2)
+    kind = part.dtype
+    vmem = pl.BlockSpec(memory_space=pltpu.VMEM)
+    dma = pltpu.SemaphoreType.DMA
+    return pl.pallas_call(
+        exchange_kernel,
+        out_shape=jax.ShapeDtypeStruct((2,) + grid + (rows, width), kind),
+        in_specs=[vmem] * 2,
+        out_specs=vmem,
+        scratch_shapes=[
+            pltpu.VMEM((2, LINE, 2, 2, rows, width), kind),
+            pltpu.VMEM((2, LINE, 2, 2, rows, half), kind),
+            pltpu.VMEM((2, LINE, 2, 2, rows, half), kind),
+            pltpu.VMEM((2, LINE, 2, rows, half), kind),
+            pltpu.VMEM((2, LINE, 2, rows, half), kind),
+            pltpu.VMEM((2, LINE - 1, 2, rows, half), kind),
+            pltpu.VMEM((2, LINE - 1, 2, rows, half), kind),
+            dma((LINE,)),
+            dma((LINE,)),
+            dma((2, LINE)),
+            dma((2, LINE)),
+            dma((2, LINE)),
+            dma((2, LINE)),
+            dma((2, LINE - 1)),
+            dma((2, LINE - 1)),
+            dma((2 * SPREAD_SENDS,)),
+            dma((2,) + grid),
+        ],
+        compiler_params=pltpu.CompilerParams(
+            collective_id=1, has_side_effects=True, vmem_limit_bytes=VMEM_BYTES
+        ),
+    )(part, targets)
+
+
+def dense_body(tokens, targets, expert_ids, gate_codes, projections, down_weight, direction):
+    tok_rows, model_width = tokens.shape
+    top_count = expert_ids.shape[1]
+    expert = lax.axis_index("expert")
+    lanes = jnp.arange(128, dtype=jnp.int32)
+    named = expert_ids[:, :, None] == lanes[None, None, :]
+    table = jnp.sum(jnp.where(named, gate_codes[:, :, None], 0), axis=1)
+    table = (table.astype(jnp.float32) / 256.0).astype(jnp.bfloat16)
+    all_tok, all_table = gather_tokens(tokens, table)
+    grid = all_tok.shape[:4]
+    all_tok = all_tok.reshape(-1, model_width)
+    weight = jnp.sum(
+        jnp.where(lanes[None, :] == expert, all_table.reshape(-1, 128).astype(jnp.float32), 0.0),
+        axis=1,
+        keepdims=True,
+    )
+    dot = functools.partial(jnp.einsum, preferred_element_type=jnp.float32)
+    gate_pre = dot("td,df->tf", all_tok, projections[0, 0])
+    up_pre = dot("td,df->tf", all_tok, projections[0, 1])
+    tangent_pre = dot("td,df->tf", all_tok, direction[0])
+    sigmoid_val = jax.nn.sigmoid(gate_pre)
+    first_slope = sigmoid_val * (1.0 + gate_pre * (1.0 - sigmoid_val))
+    second_slope = sigmoid_val * (1.0 - sigmoid_val) * (2.0 + gate_pre * (1.0 - 2.0 * sigmoid_val))
+    hidden = (weight * gate_pre * sigmoid_val * up_pre).astype(jnp.bfloat16)
+    hidden_tan = (weight * first_slope * tangent_pre * up_pre).astype(jnp.bfloat16)
+    part = dot("ktf,fd->ktd", jnp.stack([hidden, hidden_tan]), down_weight[0])
+    part = part.astype(jnp.bfloat16).reshape((2,) + grid + (tok_rows, model_width))
+    back = exchange(part, targets).reshape(2, -1, model_width)
+    grad = dot("ktd,fd->ktf", back, down_weight[0])
+    hess_pre = (
+        weight * (grad[1] * up_pre * first_slope + grad[0] * up_pre * second_slope * tangent_pre)
+    ).astype(jnp.bfloat16)
+    total = dot("td,tf->df", all_tok, hess_pre)
+    loss_scale = 1.0 / math.sqrt(tok_rows * top_count)
+    return (total * loss_scale).astype(jnp.bfloat16)[None]
 
 
 def slot_tables(route_ids, expert_total, slot_cap):
@@ -24,7 +336,7 @@
     return (landing, source_route, occupied)
 
 
-def body(tokens, targets, expert_ids, gate_codes, projections, down_weight, direction):
+def routed_body(tokens, targets, expert_ids, gate_codes, projections, down_weight, direction):
     tok_rows, model_width = tokens.shape
     top_count = expert_ids.shape[1]
     local_experts = projections.shape[0]
@@ -90,9 +402,24 @@
     return (summed * loss_scale).astype(jnp.bfloat16)
 
 
+def plan(mesh):
+    shape = dict(mesh.shape)
+    fits = shape["groups"] == 1 and shape["expert"] == LINE * 4 and shape["dp"] == 2
+
+    def body(tokens, targets, expert_ids, gate_codes, projections, down_weight, direction):
+        everyone = shape["expert"] * shape["dp"] * tokens.size * tokens.dtype.itemsize
+        dense = fits and projections.shape[0] == 1 and everyone * 2 <= DENSE_BYTES
+        chosen = dense_body if dense else routed_body
+        return chosen(
+            tokens, targets, expert_ids, gate_codes, projections, down_weight, direction
+        )
+
+    return body
+
+
 def solution(mesh):
     return jax.shard_map(
-        body,
+        plan(mesh),
         mesh=mesh,
         in_specs=(
             P(("groups", "expert", "dp"), None),

time: 393 us -> 153 us (0.39)
  waiting for transfers between devices: 205 us -> 0 us
  Pallas kernels: 0 us -> 123 us
  blocking collectives: 82.2 us -> 0 us
  local copies, waits for them, and re-layouts: 58.9 us -> 1.74 us
  between operations: 13.5 us -> 0.13 us
  other arithmetic: 12.1 us -> 2.5 us
  matrix products: 15.1 us -> 22.6 us
  starting transfers between devices: 5.92 us -> 0 us
    all_gather x3 -> x0, waiting for transfers between devices: 128 us -> none  [the longest x1 78.8 us: body(): lax.all_gather(projections, 'dp', axis=3, tiled=True)]
    pallas_call x0 -> x2, Pallas kernels: none -> 123 us  [the longest x1 91.8 us: exchange(): pl.pallas_call(exchange_kernel, out_shape=jax.ShapeDtypeStruct((2,) + gri...]
    all_to_all x2 -> x0, blocking collectives: 82.2 us -> none  [the longest x1 50.2 us: body(): lax.all_to_all(outgoing, 'expert', split_axis=1, concat_axis=1, tiled=True)]
    unnamed x5 -> x0, waiting for transfers between devices: 43.3 us -> none
    all_to_all x1 -> x0, waiting for transfers between devices: 33.9 us -> none  [body(): lax.all_to_all(expert_out, 'expert', split_axis=1, concat_axis=1, tiled=T...]
    unnamed x27 -> x10, local copies, waits for them, and re-layouts: 27.4 us -> 1.65 us
    gather x5 -> x0, local copies, waits for them, and re-layouts: 24.9 us -> none  [the longest x1 10.9 us: body(): pair_res[:, source_token] * slot_weight[None, :, None]]
    convert_element_type x4 -> x1, other arithmetic: 8.27 us -> 0.6 us  [dense_body(): table = (table.astype(jnp.float32) / 256.0).astype(jnp.bfloat16)]
  transfers between devices with their start and end apart: 5 -> 0, of which waited for: 5 -> 0; matrix products, arithmetic and copies ran while one was open for 4% -> 0% of each run, Pallas kernels for 0% -> 0%
where the time goes in v1:
time: 153 us; the launch traced here: 150 us
  Pallas kernels  123 us (80%)
  matrix products  22.6 us (15%)
  other arithmetic  2.5 us (2%)
  local copies, waits for them, and re-layouts  1.74 us (1%)
    pallas_call x1, Pallas kernels, exchange(): pl.pallas_call(exchange_kernel, out_shape=jax.ShapeDtypeStruct((2,) + gri...  91.8 us
    pallas_call x1, Pallas kernels, gather_tokens(): pl.pallas_call(gather_kernel, out_shape=(jax.ShapeDtypeStruct(grid + (row...  30.9 us
    dot_general x1, matrix products, dense_body(): grad = dot('ktd,fd->ktf', back, down_weight[0])  5.69 us
    dot_general x1, matrix products, dense_body(): part = dot('ktf,fd->ktd', jnp.stack([hidden, hidden_tan]), down_weight[0])  5.53 us
    dot_general x1, matrix products, dense_body(): tangent_pre = dot('td,df->tf', all_tok, direction[0])  4.29 us
    dot_general x1, matrix products, dense_body(): total = dot('td,tf->df', all_tok, hess_pre)  3.55 us

profile of v1, /device:TPU:0, one launch (start us, length us, event | category | flops | bytes accessed | tf_op | source)
XLA Modules:
  0.0 149.6 jit_solution(13976307450967191341)
XLA Ops:
  0.0 0.0 copy-start
  0.0 0.9 copy.10
  0.9 0.8 copy.11
  1.6 0.1 select_reduce_fusion.1
  1.8 0.6 multiply_convert_fusion.3.weight_ref
  2.4 30.9 %shard_map.73 = (bf16[4,2,2,2,24,2048]{5,4,3,2,1,0:T(8,128)(2,1)}, bf16[4,2,2,2,24,128]{5,4,3,2,1,0:T(8,128)(2,1)}) custom-call(bf16[24,2048]{1,0:T(8,128)(2,1)} %tok_ref.1, bf16[24,128]{1,0:T(8,128)(2,1)} %multiply_convert_fusion.3.weight_ref), custom_call_target="tpu_custom_call" | custom-call | tf_op jit(solution)/shard_map/pallas_call | solution.py:141
  33.2 1.1 select_reduce_fusion
  34.4 0.1 mul.73
  34.5 0.0 copy-start.1
  34.5 0.0 copy-start.2
  34.5 4.3 %fusion.4 = f32[768,384]{1,0:T(8,128)S(1)} fusion(bf16[768,2048]{1,0:T(8,128)(2,1)} %bitcast.47, bf16[1,2048,384]{2,1,0:T(8,128)(2,1)} %param.13), kind=kOutput, calls=%fused_computation.8 | convolution fusion | flops 1207959552 | bytes 5898240 | tf_op jit(solution)/shard_map/td,df->tf/dot_general | solution.py:303
  38.8 0.0 copy-done.1
  38.8 0.0 copy-done.2
  38.8 1.8 %fusion.6 = f32[768,384]{1,0:T(8,128)S(1)} fusion(bf16[768,2048]{1,0:T(8,128)(2,1)S(1)} %bitcast.48, bf16[1,2,2048,384]{3,2,1,0:T(8,128)(2,1)S(1)} %copy-done.1), kind=kOutput, calls=%fused_computation.10 | convolution fusion | flops 1207959552 | bytes 5898240 | tf_op jit(solution)/shard_map/td,df->tf/dot_general | solution.py:302
  40.6 1.8 %fusion.8 = f32[768,384]{1,0:T(8,128)S(1)} fusion(bf16[768,2048]{1,0:T(8,128)(2,1)S(1)} %bitcast.49, bf16[1,2,2048,384]{3,2,1,0:T(8,128)(2,1)S(1)} %copy-done.1), kind=kOutput, calls=%fused_computation.12 | convolution fusion | flops 1207959552 | bytes 5898240 | tf_op jit(solution)/shard_map/td,df->tf/dot_general | solution.py:301
  42.4 0.7 fusion.26
  43.0 0.0 copy-done
  43.0 5.5 %convolution_convert_fusion = bf16[2,768,2048]{2,1,0:T(8,128)(2,1)} fusion(bf16[1,384,2048]{2,1,0:T(8,128)(2,1)S(1)} %copy-done, bf16[1,768,384]{2,1,0:T(8,128)(2,1)S(1)} %get-tuple-element.10, bf16[1,768,384]{2,1,0:T(8,128)(2,1)S(1)} %get-tuple-element.9), kind=kOutput, calls=%fused_computation | convolution fusion | flops 2419654656 | bytes 9043968 | tf_op jit(solution)/shard_map/ktf,fd->ktd/dot_general | solution.py:309
  48.6 91.8 %shard_map.74 = bf16[2,4,2,2,2,24,2048]{6,5,4,3,2,1,0:T(8,128)(2,1)} custom-call(bf16[2,4,2,2,2,24,2048]{6,5,4,3,2,1,0:T(8,128)(2,1)} %bitcast.45, bf16[24,2048]{1,0:T(8,128)(2,1)} %targets.1), custom_call_target="tpu_custom_call" | custom-call | tf_op jit(solution)/shard_map/pallas_call | solution.py:254
  140.4 0.0 copy-start.3
  140.4 5.7 %fusion.1 = f32[2,768,384]{2,1,0:T(8,128)S(1)} fusion(bf16[2,768,2048]{2,1,0:T(8,128)(2,1)} %bitcast.46, bf16[1,384,2048]{2,1,0:T(8,128)(2,1)S(1)} %copy-done), kind=kOutput, calls=%fused_computation.5 | convolution fusion | flops 2415919104 | bytes 10223616 | tf_op jit(solution)/shard_map/ktd,fd->ktf/dot_general | solution.py:312
  146.1 0.0 copy-done.3
  146.1 3.5 %fusion = bf16[1,2048,384]{2,1,0:T(8,128)(2,1)} fusion(bf16[768,2048]{1,0:T(8,128)(2,1)S(1)} %bitcast.50, f32[768,384]{1,0:T(8,128)S(1)} %fusion.4, f32[768,384]{1,0:T(8,128)S(1)} %fusion.6, f32[2,768,384]{2,1,0:T(8,128)S(1)} %fusion.1, f32[768,384]{1,0:T(8,128)S(1)} %fusion.8, f32[768]{0:T(1024)S(1)} %mul.73), kind=kOutput, calls=%fused_computation.2 | convolution fusion | flops 1215725568 | bytes 10619904 | tf_op jit(solution)/shard_map/td,tf->df/dot_general | solution.py:316
  (1 shorter events, 0.0 us)
Async XLA Ops:
  0.0 43.0 %copy-start = (bf16[1,384,2048]{2,1,0:T(8,128)(2,1)S(1)}, bf16[1,384,2048]{2,1,0:T(8,128)(2,1)}, u32[]{:S(2)}) copy-start(bf16[1,384,2048]{2,1,0:T(8,128)(2,1)} %param.12) | copy-start | bytes 4718596
  34.5 4.3 %copy-start.1 = (bf16[1,2,2048,384]{3,2,1,0:T(8,128)(2,1)S(1)}, bf16[1,2,2048,384]{3,2,1,0:T(8,128)(2,1)}, u32[]{:S(2)}) copy-start(bf16[1,2,2048,384]{3,2,1,0:T(8,128)(2,1)} %param.11) | copy-start | bytes 9437188
  34.5 4.3 %copy-start.2 = (bf16[4,2,2,2,24,2048]{5,4,3,2,1,0:T(8,128)(2,1)S(1)}, bf16[4,2,2,2,24,2048]{5,4,3,2,1,0:T(8,128)(2,1)}, u32[]{:S(2)}) copy-start(bf16[4,2,2,2,24,2048]{5,4,3,2,1,0:T(8,128)(2,1)} %get-tuple-element.7) | copy-start | bytes 9437188
  140.4 5.7 %copy-start.3 = (bf16[4,2,2,2,24,2048]{5,4,3,2,1,0:T(8,128)(2,1)S(1)}, bf16[4,2,2,2,24,2048]{5,4,3,2,1,0:T(8,128)(2,1)}, u32[]{:S(2)}) copy-start(bf16[4,2,2,2,24,2048]{5,4,3,2,1,0:T(8,128)(2,1)} %get-tuple-element.7) | copy-start | bytes 9437188

commit v2 on v0

--- a/solution.py
+++ b/solution.py
@@ -1,9 +1,414 @@
+import functools
 import math
 
 import jax
 import jax.numpy as jnp
 from jax import lax
+from jax.experimental import pallas as pl
+from jax.experimental.pallas import tpu as pltpu
 from jax.sharding import PartitionSpec as P
+
+LINE = 4
+VMEM_BYTES = 56 * 1024 * 1024
+DENSE_BYTES = 16 * 1024 * 1024
+
+
+class Place:
+    def __init__(self):
+        expert = lax.axis_index("expert")
+        self.z = expert // 4
+        self.y = lax.rem(expert // 2, 2)
+        self.c = lax.rem(expert, 2)
+        self.x = lax.axis_index("dp")
+
+    def line(self, d):
+        return lax.rem(self.z + d, LINE)
+
+    def device(self, z, y, c, x):
+        return {"expert": (z * 2 + y) * 2 + c, "dp": x}
+
+    def along_z(self, d):
+        return self.device(self.line(d), self.y, self.c, self.x)
+
+    def along_y(self):
+        return self.device(self.z, 1 - self.y, self.c, self.x)
+
+    def along_x(self):
+        return self.device(self.z, self.y, self.c, 1 - self.x)
+
+    def sibling(self):
+        return self.device(self.z, self.y, 1 - self.c, self.x)
+
+    def greet(self):
+        barrier = pltpu.get_barrier_semaphore()
+        others = [self.along_z(d) for d in range(1, LINE)]
+        others += [self.along_y(), self.along_x(), self.sibling()]
+        for other in others:
+            pl.semaphore_signal(
+                barrier, inc=1, device_id=other, device_id_type=pl.DeviceIdType.MESH
+            )
+        pl.semaphore_wait(barrier, len(others))
+
+
+def remote(src, dst, send_sem, recv_sem, to):
+    return pltpu.make_async_remote_copy(
+        src_ref=src,
+        dst_ref=dst,
+        send_sem=send_sem,
+        recv_sem=recv_sem,
+        device_id=to,
+        device_id_type=pl.DeviceIdType.MESH,
+    )
+
+
+class Spread:
+    def __init__(self, me, pieces, send_sem, recv_sem):
+        self.me, self.pieces = me, pieces
+        self.send_sem, self.recv_sem = send_sem, recv_sem
+        self.sends = []
+        self.ways = [
+            (me.along_y(), me.along_x()) if first == "y" else (me.along_x(), me.along_y())
+            for _, first in pieces
+        ]
+
+    def copy(self, p, block, to, number):
+        ref = self.pieces[p][0](*block)
+        return remote(ref, ref, self.send_sem.at[number], self.recv_sem.at[(p,) + block], to)
+
+    def push(self, p, block, to):
+        item = self.copy(p, block, to, len(self.sends))
+        item.start()
+        self.sends.append(item)
+
+    def arrive(self, p, block):
+        self.copy(p, block, self.me.sibling(), 0).wait_recv()
+
+    def blocks(self, p, d):
+        me, z = self.me, self.me.line(d)
+        own = (z, me.y, me.c, me.x)
+        by_y = (z, 1 - me.y, me.c, me.x)
+        by_x = (z, me.y, me.c, 1 - me.x)
+        both = (z, 1 - me.y, me.c, 1 - me.x)
+        return (own, by_y, by_x, both) if self.pieces[p][1] == "y" else (own, by_x, by_y, both)
+
+    def start(self):
+        for d in range(LINE - 1, 0, -1):
+            for p in range(len(self.pieces)):
+                self.push(p, self.blocks(p, 0)[0], self.me.along_z(d))
+
+    def line_step(self, d):
+        for p in range(len(self.pieces)):
+            block = self.blocks(p, d)[0]
+            if d:
+                self.arrive(p, block)
+            self.push(p, block, self.ways[p][0])
+            self.push(p, block, self.ways[p][1])
+            self.push(p, block, self.me.sibling())
+
+    def first_step(self, d):
+        for p in range(len(self.pieces)):
+            block = self.blocks(p, d)[1]
+            self.arrive(p, block)
+            self.push(p, block, self.ways[p][1])
+            self.push(p, block, self.me.sibling())
+
+    def second_step(self, d):
+        for p in range(len(self.pieces)):
+            for block in self.blocks(p, d)[2:]:
+                self.arrive(p, block)
+                self.push(p, block, self.me.sibling())
+
+    def core_step(self, d):
+        for p in range(len(self.pieces)):
+            for y in range(2):
+                for x in range(2):
+                    self.arrive(p, (self.me.line(d), y, 1 - self.me.c, x))
+
+    def finish(self):
+        for item in self.sends:
+            item.wait_send()
+
+
+SPREAD_SENDS = 3 + LINE * 5 + LINE * 2
+
+
+def rows_of(block):
+    return block.reshape(-1, block.shape[-1])
+
+
+def dot(a, b, dims=((1,), (0,))):
+    return lax.dot_general(a, b, (dims, ((), ())), preferred_element_type=jnp.float32)
+
+
+def fused_kernel(
+    loss_scale, tok_ref, table_ref, targets, proj_hbm, down_hbm, dir_hbm, hvp_ref,
+    all_tok, all_table, proj, down, direction, slope_a, slope_b,
+    part, back, total_hvp, core_in, out1, in1, out2, in2, out3, in3,
+    weight_sem, core_send, core_recv, send1, recv1, send2, recv2, send3, recv3,
+    tok_send, tok_recv, back_send, back_recv,
+):
+    me = Place()
+    expert = lax.axis_index("expert")
+    half = tok_ref.shape[1] // 2
+    loads = [
+        pltpu.make_async_copy(proj_hbm.at[0], proj, weight_sem.at[0]),
+        pltpu.make_async_copy(dir_hbm.at[0], direction, weight_sem.at[1]),
+        pltpu.make_async_copy(down_hbm.at[0], down, weight_sem.at[2]),
+    ]
+    for load in loads:
+        load.start()
+    all_tok[me.z, me.y, me.c, me.x] = tok_ref[...]
+    all_table[me.z, me.y, me.c, me.x] = table_ref[...]
+    me.greet()
+    tok = Spread(
+        me,
+        [
+            (lambda z, y, c, x: all_tok.at[z, y, c, x, :, pl.ds(0, half)], "y"),
+            (lambda z, y, c, x: all_tok.at[z, y, c, x, :, pl.ds(half, half)], "x"),
+            (lambda z, y, c, x: all_table.at[z, y, c, x], "y"),
+        ],
+        tok_send,
+        tok_recv,
+    )
+    sends = []
+
+    def push(src, dst, send, recv, to):
+        item = remote(src, dst, send, recv, to)
+        item.start()
+        sends.append(item)
+        return item
+
+    def forward(d):
+        z = me.line(d)
+        rows = rows_of(all_tok[z])
+        gate_pre = dot(rows, proj[0])
+        up_pre = dot(rows, proj[1])
+        tangent_pre = dot(rows, direction[...])
+        table = rows_of(all_table[z].astype(jnp.float32))
+        named = lax.broadcasted_iota(jnp.int32, table.shape, 1) == expert
+        weight = jnp.sum(jnp.where(named, table, 0.0), axis=1, keepdims=True)
+        sig = jax.nn.sigmoid(gate_pre)
+        rest = 1.0 - sig
+        up_weighted = weight * up_pre
+        slope = up_weighted * (sig * (1.0 + gate_pre * rest))
+        curve = up_weighted * (sig * rest * (2.0 + gate_pre * (1.0 - 2.0 * sig))) * tangent_pre
+        slope_a[d] = slope
+        slope_b[d] = curve
+        hidden = (gate_pre * sig * up_weighted).astype(jnp.bfloat16)
+        hidden_tan = (slope * tangent_pre).astype(jnp.bfloat16)
+        if d == 0:
+            loads[2].wait()
+        for k, value in enumerate((hidden, hidden_tan)):
+            out = dot(value, down[...]).reshape(part.shape[2:])
+            part[k, z] = out.astype(part.dtype)
+
+    core_copies, first, second, third = {}, {}, {}, {}
+
+    def core_send_step(d):
+        z = me.line(d)
+        core_copies[d] = push(
+            part.at[:, z, :, 1 - me.c], core_in.at[:, z], core_send.at[d], core_recv.at[d],
+            me.sibling(),
+        )
+
+    def pair(h, z, far, near):
+        cols = pl.ds(h * half, half)
+        y, x = (near, far) if h == 0 else (far, near)
+        mine = part[:, z, y, me.c, x, :, cols].astype(jnp.float32)
+        return mine + core_in[:, z, y, x, :, cols].astype(jnp.float32)
+
+    axis1 = (me.along_x(), me.along_y())
+    axis2 = (me.along_y(), me.along_x())
+    far_own = (me.x, me.y)
+    near_own = (me.y, me.x)
+
+    def sum_first(d):
+        core_copies[d].wait_recv()
+        for h in range(2):
+            for near in range(2):
+                out1[h, d, near] = pair(h, me.line(d), 1 - far_own[h], near).astype(out1.dtype)
+            first[d, h] = push(
+                out1.at[h, d], in1.at[h, d], send1.at[h, d], recv1.at[h, d], axis1[h]
+            )
+
+    def sum_second(d):
+        for h in range(2):
+            first[d, h].wait_recv()
+            near = 1 - near_own[h]
+            total = pair(h, me.line(d), far_own[h], near) + in1[h, d, near].astype(jnp.float32)
+            out2[h, d] = total.astype(out2.dtype)
+            second[d, h] = push(
+                out2.at[h, d], in2.at[h, d], send2.at[h, d], recv2.at[h, d], axis2[h]
+            )
+
+    def plane_total(d, h):
+        second[d, h].wait_recv()
+        near = near_own[h]
+        total = pair(h, me.line(d), far_own[h], near) + in1[h, d, near].astype(jnp.float32)
+        return total + in2[h, d].astype(jnp.float32)
+
+    def sum_third(d):
+        for h in range(2):
+            out3[h, d - 1] = plane_total(d, h).astype(out3.dtype)
+            third[d, h] = push(
+                out3.at[h, d - 1], in3.at[h, d - 1], send3.at[h, d - 1], recv3.at[h, d - 1],
+                me.along_z(d),
+            )
+
+    tok.start()
+    tok.line_step(0)
+    tok.first_step(0)
+    tok.line_step(1)
+    tok.second_step(0)
+    tok.first_step(1)
+    tok.core_step(0)
+    loads[0].wait()
+    loads[1].wait()
+    forward(0)
+    core_send_step(0)
+    tok.line_step(2)
+    tok.second_step(1)
+    tok.first_step(2)
+    tok.core_step(1)
+    sum_first(0)
+    tok.line_step(3)
+    forward(1)
+    core_send_step(1)
+    tok.first_step(3)
+    tok.second_step(2)
+    tok.core_step(2)
+    sum_first(1)
+    sum_second(0)
+    forward(2)
+    core_send_step(2)
+    tok.second_step(3)
+    tok.core_step(3)
+    sum_first(2)
+    sum_second(1)
+    forward(3)
+    core_send_step(3)
+    sum_third(1)
+    sum_first(3)
+    sum_second(2)
+    sum_third(2)
+    sum_second(3)
+    sum_third(3)
+
+    spread = Spread(
+        me,
+        [
+            (lambda z, y, c, x: back.at[:, z, y, c, x, :, pl.ds(0, half)], "y"),
+            (lambda z, y, c, x: back.at[:, z, y, c, x, :, pl.ds(half, half)], "x"),
+        ],
+        back_send,
+        back_recv,
+    )
+    for h in range(2):
+        cols = pl.ds(h * half, half)
+        total = plane_total(0, h)
+        for d in range(1, LINE):
+            third[d, h].wait_recv()
+            total = total + in3[h, d - 1].astype(jnp.float32)
+        residual = total[0] - targets[:, cols].astype(jnp.float32)
+        back[0, me.z, me.y, me.c, me.x, :, cols] = residual.astype(back.dtype)
+        back[1, me.z, me.y, me.c, me.x, :, cols] = total[1].astype(back.dtype)
+
+    def backward(d):
+        z = me.line(d)
+        grad_hidden = dot(rows_of(back[0, z]), down[...], ((1,), (1,)))
+        grad_tangent = dot(rows_of(back[1, z]), down[...], ((1,), (1,)))
+        hess_pre = (grad_tangent * slope_a[d] + grad_hidden * slope_b[d]).astype(jnp.bfloat16)
+        term = dot(rows_of(all_tok[z]), hess_pre, ((0,), (0,)))
+        if d == 0:
+            total_hvp[...] = term
+        elif d < LINE - 1:
+            total_hvp[...] += term
+        else:
+            hvp_ref[0] = ((total_hvp[...] + term) * loss_scale).astype(hvp_ref.dtype)
+
+    spread.start()
+    spread.line_step(0)
+    spread.first_step(0)
+    spread.line_step(1)
+    spread.second_step(0)
+    spread.first_step(1)
+    spread.core_step(0)
+    spread.line_step(2)
+    backward(0)
+    spread.second_step(1)
+    spread.first_step(2)
+    spread.core_step(1)
+    spread.line_step(3)
+    backward(1)
+    spread.first_step(3)
+    spread.second_step(2)
+    spread.core_step(2)
+    backward(2)
+    spread.second_step(3)
+    spread.core_step(3)
+    backward(3)
+    tok.finish()
+    spread.finish()
+    for item in sends:
+        item.wait_send()
+
+
+def dense_body(tokens, targets, expert_ids, gate_codes, projections, down_weight, direction):
+    rows, width = tokens.shape
+    units = down_weight.shape[1]
+    top_count = expert_ids.shape[1]
+    half = width // 2
+    grid = (LINE, 2, 2, 2)
+    plane_rows = 8 * rows
+    kind = tokens.dtype
+    lanes = jnp.arange(128, dtype=jnp.int32)
+    named = expert_ids[:, :, None] == lanes[None, None, :]
+    table = jnp.sum(jnp.where(named, gate_codes[:, :, None], 0), axis=1)
+    table = (table.astype(jnp.float32) / 256.0).astype(jnp.bfloat16)
+    vmem = pl.BlockSpec(memory_space=pltpu.VMEM)
+    hbm = pl.BlockSpec(memory_space=pl.ANY)
+    dma = pltpu.SemaphoreType.DMA
+    return pl.pallas_call(
+        functools.partial(fused_kernel, 1.0 / math.sqrt(rows * top_count)),
+        out_shape=jax.ShapeDtypeStruct((1, width, units), jnp.bfloat16),
+        in_specs=[vmem] * 3 + [hbm] * 3,
+        out_specs=vmem,
+        scratch_shapes=[
+            pltpu.VMEM(grid + (rows, width), kind),
+            pltpu.VMEM(grid + (rows, 128), kind),
+            pltpu.VMEM((2, width, units), kind),
+            pltpu.VMEM((units, width), kind),
+            pltpu.VMEM((width, units), kind),
+            pltpu.VMEM((LINE, plane_rows, units), jnp.float32),
+            pltpu.VMEM((LINE, plane_rows, units), jnp.float32),
+            pltpu.VMEM((2,) + grid + (rows, width), kind),
+            pltpu.VMEM((2,) + grid + (rows, width), kind),
+            pltpu.VMEM((width, units), jnp.float32),
+            pltpu.VMEM((2, LINE, 2, 2, rows, width), kind),
+            pltpu.VMEM((2, LINE, 2, 2, rows, half), kind),
+            pltpu.VMEM((2, LINE, 2, 2, rows, half), kind),
+            pltpu.VMEM((2, LINE, 2, rows, half), kind),
+            pltpu.VMEM((2, LINE, 2, rows, half), kind),
+            pltpu.VMEM((2, LINE - 1, 2, rows, half), kind),
+            pltpu.VMEM((2, LINE - 1, 2, rows, half), kind),
+            dma((3,)),
+            dma((LINE,)),
+            dma((LINE,)),
+            dma((2, LINE)),
+            dma((2, LINE)),
+            dma((2, LINE)),
+            dma((2, LINE)),
+            dma((2, LINE - 1)),
+            dma((2, LINE - 1)),
+            dma((3 * SPREAD_SENDS,)),
+            dma((3,) + grid),
+            dma((2 * SPREAD_SENDS,)),
+            dma((2,) + grid),
+        ],
+        compiler_params=pltpu.CompilerParams(
+            collective_id=0, has_side_effects=True, vmem_limit_bytes=VMEM_BYTES
+        ),
+    )(tokens, table, targets, projections, down_weight, direction)
 
 
 def slot_tables(route_ids, expert_total, slot_cap):
@@ -24,7 +429,7 @@
     return (landing, source_route, occupied)
 
 
-def body(tokens, targets, expert_ids, gate_codes, projections, down_weight, direction):
+def routed_body(tokens, targets, expert_ids, gate_codes, projections, down_weight, direction):
     tok_rows, model_width = tokens.shape
     top_count = expert_ids.shape[1]
     local_experts = projections.shape[0]
@@ -90,9 +495,24 @@
     return (summed * loss_scale).astype(jnp.bfloat16)
 
 
+def plan(mesh):
+    shape = dict(mesh.shape)
+    fits = shape["groups"] == 1 and shape["expert"] == LINE * 4 and shape["dp"] == 2
+
+    def body(tokens, targets, expert_ids, gate_codes, projections, down_weight, direction):
+        everyone = shape["expert"] * shape["dp"] * tokens.size * tokens.dtype.itemsize
+        dense = fits and projections.shape[0] == 1 and everyone * 2 <= DENSE_BYTES
+        chosen = dense_body if dense else routed_body
+        return chosen(
+            tokens, targets, expert_ids, gate_codes, projections, down_weight, direction
+        )
+
+    return body
+
+
 def solution(mesh):
     return jax.shard_map(
-        body,
+        plan(mesh),
         mesh=mesh,
         in_specs=(
             P(("groups", "expert", "dp"), None),

time: 393 us -> 112 us (0.28)
  waiting for transfers between devices: 205 us -> 0 us
  Pallas kernels: 0 us -> 107 us
  blocking collectives: 82.2 us -> 0 us
  local copies, waits for them, and re-layouts: 58.9 us -> 4.23 us
  matrix products: 15.1 us -> 0 us
  between operations: 13.5 us -> 0.02 us
  other arithmetic: 12.1 us -> 0.72 us
  starting transfers between devices: 5.92 us -> 0 us
    all_gather x3 -> x0, waiting for transfers between devices: 128 us -> none  [the longest x1 78.8 us: body(): lax.all_gather(projections, 'dp', axis=3, tiled=True)]
    pallas_call x0 -> x1, Pallas kernels: none -> 107 us  [dense_body(): pl.pallas_call(functools.partial(fused_kernel, 1.0 / math.sqrt(rows * top...]
    all_to_all x2 -> x0, blocking collectives: 82.2 us -> none  [the longest x1 50.2 us: body(): lax.all_to_all(outgoing, 'expert', split_axis=1, concat_axis=1, tiled=True)]
    unnamed x5 -> x0, waiting for transfers between devices: 43.3 us -> none
    all_to_all x1 -> x0, waiting for transfers between devices: 33.9 us -> none  [body(): lax.all_to_all(expert_out, 'expert', split_axis=1, concat_axis=1, tiled=T...]
    gather x5 -> x0, local copies, waits for them, and re-layouts: 24.9 us -> none  [the longest x1 10.9 us: body(): pair_res[:, source_token] * slot_weight[None, :, None]]
    unnamed x27 -> x3, local copies, waits for them, and re-layouts: 27.4 us -> 4.23 us
    dot_general x5 -> x0, matrix products: 15.1 us -> none  [the longest x1 4.5 us: body(): jnp.einsum('sxcd,xkdf->ksxcf', arrived, lax.all_gather(projections, 'dp',...]
  transfers between devices with their start and end apart: 5 -> 0, of which waited for: 5 -> 0; matrix products, arithmetic and copies ran while one was open for 4% -> 0% of each run, Pallas kernels for 0% -> 0%
where the time goes in v2:
time: 112 us
  Pallas kernels  107 us (96%)
  local copies, waits for them, and re-layouts  4.23 us (4%)
    pallas_call x1, Pallas kernels, dense_body(): pl.pallas_call(functools.partial(fused_kernel, 1.0 / math.sqrt(rows * top...  107 us
    unnamed x3, local copies, waits for them, and re-layouts  4.23 us

profile of v2, /device:TPU:0, one launch (start us, length us, event | category | flops | bytes accessed | tf_op | source)
XLA Modules:
  0.0 112.2 jit_solution(2274377309661474992)
XLA Ops:
  0.0 0.8 copy.10
  0.8 0.8 copy.11
  1.5 0.1 select_reduce_fusion
  1.6 0.6 multiply_convert_fusion.table_ref
  2.2 107.2 %shard_map.73 = bf16[1,2048,384]{2,1,0:T(8,128)(2,1)} custom-call(bf16[24,2048]{1,0:T(8,128)(2,1)} %tok_ref.1, bf16[24,128]{1,0:T(8,128)(2,1)} %multiply_convert_fusion.table_ref, bf16[24,2048]{1,0:T(8,128)(2,1)} %targets.1, bf16[1,2,2048,384]{3,2,1,0:T(8,128)(2,1)} %proj_hbm.1, bf16[1,384,2048]{2,1,0:T(8,128)(2,1)} %down_hbm.1, bf16[1,2048,384]{2,1,0:T(8,128)(2,1)} %dir_hbm.1), custom_call_target="tpu_custom_call" | custom-call | tf_op jit(solution)/shard_map/pallas_call | solution.py:371
  109.5 2.7 %copy.13 = bf16[1,2048,384]{2,1,0:T(8,128)(2,1)} copy(bf16[1,2048,384]{2,1,0:T(8,128)(2,1)} %shard_map.73) | data formatting | bytes 3145728

commit v3 on v2

--- a/solution.py
+++ b/solution.py
@@ -270,15 +270,13 @@
     tok.second_step(1)
     tok.first_step(2)
     tok.core_step(1)
-    sum_first(0)
-    tok.line_step(3)
     forward(1)
     core_send_step(1)
+    tok.line_step(3)
+    tok.second_step(2)
     tok.first_step(3)
-    tok.second_step(2)
     tok.core_step(2)
     sum_first(1)
-    sum_second(0)
     forward(2)
     core_send_step(2)
     tok.second_step(3)
@@ -287,12 +285,14 @@
     sum_second(1)
     forward(3)
     core_send_step(3)
+    sum_first(3)
     sum_third(1)
-    sum_first(3)
     sum_second(2)
     sum_third(2)
+    sum_first(0)
     sum_second(3)
     sum_third(3)
+    sum_second(0)
 
     spread = Spread(
         me,
@@ -362,8 +362,8 @@
     plane_rows = 8 * rows
     kind = tokens.dtype
     lanes = jnp.arange(128, dtype=jnp.int32)
-    named = expert_ids[:, :, None] == lanes[None, None, :]
-    table = jnp.sum(jnp.where(named, gate_codes[:, :, None], 0), axis=1)
+    named = expert_ids.T[:, :, None] == lanes[None, None, :]
+    table = jnp.sum(jnp.where(named, gate_codes.T[:, :, None], 0), axis=0)
     table = (table.astype(jnp.float32) / 256.0).astype(jnp.bfloat16)
     vmem = pl.BlockSpec(memory_space=pltpu.VMEM)
     hbm = pl.BlockSpec(memory_space=pl.ANY)

time: 112 us -> 107 us (0.955)
  Pallas kernels: 107 us -> 103 us
  local copies, waits for them, and re-layouts: 4.23 us -> 2.71 us
    pallas_call x1, Pallas kernels: 107 us -> 103 us  [dense_body(): pl.pallas_call(functools.partial(fused_kernel, 1.0 / math.sqrt(rows * top...]
    unnamed x3 -> x1, local copies, waits for them, and re-layouts: 4.23 us -> 2.71 us
where the time goes in v3:
time: 107 us
  Pallas kernels  103 us (96%)
  local copies, waits for them, and re-layouts  2.71 us (3%)
  other arithmetic  1.42 us (1%)
    pallas_call x1, Pallas kernels, dense_body(): pl.pallas_call(functools.partial(fused_kernel, 1.0 / math.sqrt(rows * top...  103 us
    unnamed x1, local copies, waits for them, and re-layouts  2.71 us

profile of v3, /device:TPU:0, one launch (start us, length us, event | category | flops | bytes accessed | tf_op | source)
XLA Modules:
  0.0 107.0 jit_solution(16394568290529047752)
XLA Ops:
  0.0 0.8 select_reduce_fusion
  0.8 0.6 multiply_convert_fusion.table_ref
  1.4 102.9 %shard_map.73 = bf16[1,2048,384]{2,1,0:T(8,128)(2,1)} custom-call(bf16[24,2048]{1,0:T(8,128)(2,1)} %tok_ref.1, bf16[24,128]{1,0:T(8,128)(2,1)} %multiply_convert_fusion.table_ref, bf16[24,2048]{1,0:T(8,128)(2,1)} %targets.1, bf16[1,2,2048,384]{3,2,1,0:T(8,128)(2,1)} %proj_hbm.1, bf16[1,384,2048]{2,1,0:T(8,128)(2,1)} %down_hbm.1, bf16[1,2048,384]{2,1,0:T(8,128)(2,1)} %dir_hbm.1), custom_call_target="tpu_custom_call" | custom-call | tf_op jit(solution)/shard_map/pallas_call | solution.py:371
  104.3 2.7 %copy.9 = bf16[1,2048,384]{2,1,0:T(8,128)(2,1)} copy(bf16[1,2048,384]{2,1,0:T(8,128)(2,1)} %shard_map.73) | data formatting | bytes 3145728
